TPU v7x, 128 devices: a whole 4x4x4 slice. The times are simulated.
128 devices in a mesh: space: 8 (over z, y_lo), vel: 16 (over y_hi, x, core).
Axes of the slice: x: 4, y: 4 (y_hi: 2, y_lo: 2; y = y_hi * 2 + y_lo), z: 4, core: 2. Of those that a mesh axis runs over, the one named last changes fastest.
Arguments:
- distribution: bfloat16 [4096, 48, 8, 128], P('vel', 'space'), may hold values from -6 to 6
- up_factor: bfloat16 [4096, 256], P('vel'), may hold values from -0.75 to 0.75
- down_factor: bfloat16 [4096, 256], P('vel'), may hold values from -0.09375 to 0.09375
- decay: float32 [4096], P('vel'), may hold values from 0.3 to 3
- wall_kind: int32 [2, 8, 128], replicated, may hold values from 0 to 2
Outputs:
- advanced: bfloat16 [4096, 48, 8, 128], P('vel', 'space')
Inputs may be any that keep to these rules, and one draw needn't show every extreme that they name: `wall_kind`: 0 marks a diffuse wall at rest, 1 a diffuse heated wall, 2 an open face.
All inputs are finite; a program needn't handle non-finite values.
Results may differ from a plain program's by a relative error of at most 0.0046.
Values may be sent and summed in bfloat16 or wider, within the bound.
A program may use at most 192 MiB of HBM per device.

v0:
```python
import jax
import jax.numpy as jnp
from jax import lax
from jax.sharding import PartitionSpec as P

NV = 16
STEPS = 2
speed_range = 8.0
time_ratio = 0.08
wall_heat = 3.0


def with_halo(block, sides, width):
    for axis, dim in sides:
        count = lax.axis_size(axis)
        forward = [(i, i + 1) for i in range(count - 1)]
        backward = [(target, source) for source, target in forward]
        low = lax.ppermute(
            lax.slice_in_dim(block, block.shape[dim] - width, None, axis=dim), axis, forward
        )
        high = lax.ppermute(lax.slice_in_dim(block, 0, width, axis=dim), axis, backward)
        block = jnp.concatenate([low, block, high], axis=dim)
    return block


def components(vel_ids):
    spacing = speed_range / NV
    midpoint = (NV - 1) / 2.0
    along_z = ((vel_ids // (NV * NV)).astype(jnp.float32) - midpoint) * spacing
    along_x = ((vel_ids // NV % NV).astype(jnp.float32) - midpoint) * spacing
    along_y = ((vel_ids % NV).astype(jnp.float32) - midpoint) * spacing
    return (along_z, along_x, along_y)


def wall_ghost(outflux, kind_face, maxwell, energy, norm):
    sigma = outflux / norm
    heating = jnp.where(kind_face == 1, wall_heat, 0.0)
    opened = jnp.where(kind_face == 2, 0.0, 1.0)
    return (
        maxwell[:, None, None]
        * (sigma[None] + heating[None] * energy[:, None, None])
        * opened[None]
    )


def transport(centre, lower_plane, upper_plane, along_z, along_x, along_y):
    dimensions = centre.ndim
    shaped = (-1,) + (1,) * (dimensions - 1)
    axis_x = dimensions - 2
    axis_y = dimensions - 1
    plus_z = jnp.maximum(along_z, 0.0).reshape(shaped)
    minus_z = jnp.minimum(along_z, 0.0).reshape(shaped)
    plus_x = jnp.maximum(along_x, 0.0).reshape(shaped)
    minus_x = jnp.minimum(along_x, 0.0).reshape(shaped)
    plus_y = jnp.maximum(along_y, 0.0).reshape(shaped)
    minus_y = jnp.minimum(along_y, 0.0).reshape(shaped)
    result = plus_z * (centre - lower_plane) + minus_z * (upper_plane - centre)
    result = (
        result
        + plus_x * (centre - jnp.roll(centre, 1, axis_x))
        + minus_x * (jnp.roll(centre, -1, axis_x) - centre)
    )
    result = (
        result
        + plus_y * (centre - jnp.roll(centre, 1, axis_y))
        + minus_y * (jnp.roll(centre, -1, axis_y) - centre)
    )
    return result


def body(distribution, up_factor, down_factor, decay, wall_kind):
    local_vel, depth, width_x, width_y = distribution.shape
    cells = depth * width_x * width_y
    vel_ids = lax.axis_index("vel") * local_vel + jnp.arange(local_vel, dtype=jnp.int32)
    along_z, along_x, along_y = components(vel_ids)
    speed_sq = along_z * along_z + along_x * along_x + along_y * along_y
    maxwell = jnp.exp(-0.5 * speed_sq)
    energy = 0.5 * speed_sq - 1.5
    all_ids = jnp.arange(NV**3, dtype=jnp.int32)
    full_z, full_x, full_y = components(all_ids)
    norm = jnp.sum(
        jnp.maximum(full_z, 0.0)
        * jnp.exp(-0.5 * (full_z * full_z + full_x * full_x + full_y * full_y))
    )
    slab = lax.axis_index("space")
    slabs = lax.axis_size("space")
    current = distribution
    for step in range(STEPS):
        low_face = current[:, 0].astype(jnp.float32)
        high_face = current[:, depth - 1].astype(jnp.float32)
        out_low = jnp.sum(jnp.maximum(-along_z, 0.0)[:, None, None] * low_face, axis=0)
        out_high = jnp.sum(jnp.maximum(along_z, 0.0)[:, None, None] * high_face, axis=0)
        outflux = lax.psum(jnp.stack([out_low, out_high]), "vel")
        ghost_low = wall_ghost(outflux[0], wall_kind[0], maxwell, energy, norm)
        ghost_high = wall_ghost(outflux[1], wall_kind[1], maxwell, energy, norm)
        padded = with_halo(current, (("space", 1),), 1)
        first_plane = jnp.where(slab == 0, ghost_low, padded[:, 0].astype(jnp.float32))
        last_plane = jnp.where(
            slab == slabs - 1, ghost_high, padded[:, depth + 1].astype(jnp.float32)
        )
        lower_plane = jnp.concatenate(
            [first_plane[:, None], padded[:, 1:depth].astype(jnp.float32)], axis=1
        )
        upper_plane = jnp.concatenate(
            [padded[:, 2 : depth + 1].astype(jnp.float32), last_plane[:, None]], axis=1
        )
        centre = current.astype(jnp.float32)
        moved = transport(centre, lower_plane, upper_plane, along_z, along_x, along_y)
        flat_rows = current.reshape(local_vel, cells)
        coeffs = lax.psum_scatter(
            lax.dot_general(
                flat_rows, down_factor, (((0,), (0,)), ((), ())), preferred_element_type=jnp.float32
            ),
            "vel",
            scatter_dimension=0,
            tiled=True,
        ).astype(jnp.bfloat16)
        gained = lax.dot_general(
            up_factor,
            lax.all_gather(coeffs, "vel", axis=0, tiled=True),
            (((1,), (1,)), ((), ())),
            preferred_element_type=jnp.float32,
        ).reshape(current.shape)
        updated = (
            centre
            - time_ratio * moved
            + time_ratio * (gained - decay[:, None, None, None] * centre)
        )
        current = updated.astype(jnp.bfloat16)
    return current


def solution(mesh):
    return jax.shard_map(
        body,
        mesh=mesh,
        in_specs=(P("vel", "space", None, None), P("vel", None), P("vel", None), P("vel"), P()),
        out_specs=P("vel", "space", None, None),
        check_vma=False,
    )
```

profile of v0, /device:TPU:8, one launch (start us, length us, event | category | flops | bytes accessed | tf_op | source)
XLA Modules:
  0.0 419.7 jit_solution(15023858921832519522)
XLA Ops:
  7.4 5.9 %fusion.35 = f32[6144,256]{1,0:T(8,128)} fusion(bf16[256,256]{1,0:T(8,128)(2,1)S(1)} %copy-done, bf16[32,8,48,128]{3,2,1,0:T(8,128)(2,1)} %bitcast.76), kind=kOutput, calls=%fused_computation.51 | convolution fusion | flops 805306368 | bytes 9568256 | tf_op jit(solution)/shard_map/dot_general | solution.py:111
  13.4 91.1 %reduce-scatter.3.cloned.1.call-done = f32[384,256]{1,0:T(8,128)} async-done(((f32[6144,256]{1,0:T(8,128)}), f32[384,256]{1,0:T(8,128)}) %reduce-scatter.3.cloned.1.call-update) | async-done | bytes 393232 | tf_op jit(solution)/shard_map/reduce_scatter | solution.py:110
  107.4 4.3 %collective-permute-start = (bf16[256,1,8,128]{3,2,0,1:T(8,128)(2,1)}, bf16[256,1,8,128]{3,2,0,1:T(8,128)(2,1)}, u32[]{:S(2)}, u32[]{:S(2)}) collective-permute-start(bf16[256,1,8,128]{3,2,0,1:T(8,128)(2,1)} %get-tuple-element.21), channel_id=1, source_target_pairs={{0,16},{16,32},{32,48},{48,64},{64,80},{80,96},{96,112},{1,17},{17... | collective-permute-start | bytes 1572872 | tf_op jit(solution)/shard_map/ppermute | solution.py:18
  115.7 34.9 %psum.14 = f32[2,8,128]{2,1,0:T(8,128)S(1)} all-reduce(f32[2,8,128]{2,1,0:T(8,128)S(1)} %pad_maximum_fusion), channel_id=1, replica_groups=mesh['space'=8,'vel'=16] {'vel'}, use_global_device_ids=true, to_apply=%region_2.3 | all-reduce | flops 2048 | bytes 16384 | tf_op jit(solution)/shard_map/psum | solution.py:93
  150.7 4.7 %slice_convert_fusion.3 = (f32[256,5,8,128]{3,2,1,0:T(8,128)}, f32[256,5,8,128]{3,2,1,0:T(8,128)}) fusion(bf16[256,6,8,128]{3,2,1,0:T(8,128)(2,1)S(1)} %copy-done.2), kind=kLoop, calls=%fused_computation.57 | loop fusion | flops 2621440 | bytes 15728640 | tf_op jit(solution)/shard_map/convert_element_type | solution.py:102
  157.5 5.5 %fusion.106 = (f32[256,6,8,127]{3,2,1,0:T(8,128)}, f32[256,6,8,127]{3,2,1,0:T(8,128)}) fusion(bf16[256,6,8,128]{3,2,1,0:T(8,128)(2,1)S(1)} %copy-done.2), kind=kLoop, calls=%fused_computation.182 | loop fusion | bytes 24969216 | tf_op jit(solution)/shard_map/jit(_roll_static)/slice | solution.py:65
  163.0 5.5 %fusion.105 = (f32[256,6,8,1]{3,2,1,0:T(8,128)}, f32[256,6,8,1]{3,2,1,0:T(8,128)}) fusion(bf16[256,6,8,128]{3,2,1,0:T(8,128)(2,1)S(1)} %copy-done.2), kind=kLoop, calls=%fused_computation.181 | loop fusion | bytes 196608 | tf_op jit(solution)/shard_map/jit(_roll_static)/slice | solution.py:65
  168.5 5.4 %fusion.104 = (f32[256,6,7,128]{3,2,1,0:T(8,128)}, f32[256,6,7,128]{3,2,1,0:T(8,128)}) fusion(bf16[256,6,8,128]{3,2,1,0:T(8,128)(2,1)S(1)} %copy-done.2), kind=kLoop, calls=%fused_computation.180 | loop fusion | bytes 22020096 | tf_op jit(solution)/shard_map/jit(_roll_static)/slice | solution.py:60
  177.2 2.6 fusion.49
  179.8 5.5 %fusion.107 = f32[6144,256]{1,0:T(8,128)} fusion(bf16[6144,256]{1,0:T(8,128)(2,1)} %all-gather.3.cloned.1.call-done, bf16[256,256]{1,0:T(8,128)(2,1)S(1)} %copy-done.3), kind=kOutput, calls=%fused_computation.183 | convolution fusion | flops 805306368 | bytes 9568256 | tf_op jit(solution)/shard_map/dot_general | solution.py:118
  185.3 6.7 %copy.10 = f32[256,6,8,128]{3,2,1,0:T(8,128)} copy(f32[256,6,8,128]{0,3,2,1:T(8,128)} %bitcast.77) | data formatting | bytes 12582912 | tf_op jit(solution)/shard_map/reshape | solution.py:123
  192.0 21.8 %fusion.31 = bf16[256,6,8,128]{3,2,1,0:T(8,128)(2,1)S(1)} fusion(f32[256,6,8,128]{3,2,1,0:T(8,128)} %copy.10, f32[256,6,8,1]{3,2,1,0:T(8,128)} %get-tuple-element.30, f32[256,6,8,127]{3,2,1,0:T(8,128)} %get-tuple-element.32, f32[256,6,8,127]{3,2,1,0:T(8,128)} %get-tuple-element.31, f32[256,6,8,1]{3,2,1,0:T(8,128)} %get-tuple-element.29, ...), kind=kLoop, calls=%fused_computation.47 | loop fusion | flops 48758784 | bytes 50338816 | tf_op jit(solution)/shard_map/convert_element_type | solution.py:129
  213.8 4.0 fusion.32
  217.8 87.7 %reduce-scatter.5.cloned.1.call-done = f32[384,256]{1,0:T(8,128)} async-done(((f32[6144,256]{1,0:T(8,128)}), f32[384,256]{1,0:T(8,128)}) %reduce-scatter.5.cloned.1.call-update) | async-done | bytes 393232 | tf_op jit(solution)/shard_map/reduce_scatter | solution.py:110
  308.3 4.3 %collective-permute-start.2 = (bf16[256,1,8,128]{3,2,0,1:T(8,128)(2,1)}, bf16[256,1,8,128]{3,2,0,1:T(8,128)(2,1)}, u32[]{:S(2)}, u32[]{:S(2)}) collective-permute-start(bf16[256,1,8,128]{3,2,0,1:T(8,128)(2,1)} %get-tuple-element.9), channel_id=1, source_target_pairs={{0,16},{16,32},{32,48},{48,64},{64,80},{80,96},{96,112},{1,17},{17... | collective-permute-start | bytes 1572872 | tf_op jit(solution)/shard_map/ppermute | solution.py:18
  316.0 35.1 %psum.15 = f32[2,8,128]{2,1,0:T(8,128)S(1)} all-reduce(f32[2,8,128]{2,1,0:T(8,128)S(1)} %pad_maximum_fusion.1), channel_id=1, replica_groups=mesh['space'=8,'vel'=16] {'vel'}, use_global_device_ids=true, to_apply=%region_7.8 | all-reduce | flops 2048 | bytes 16384 | tf_op jit(solution)/shard_map/psum | solution.py:93
  353.8 5.6 %fusion.102 = (f32[256,6,8,127]{3,2,1,0:T(8,128)}, f32[256,6,8,127]{3,2,1,0:T(8,128)}) fusion(bf16[256,6,8,128]{3,2,1,0:T(8,128)(2,1)S(1)} %fusion.31), kind=kLoop, calls=%fused_computation.178 | loop fusion | bytes 24969216 | tf_op jit(solution)/shard_map/jit(_roll_static)/slice | solution.py:65
  359.4 5.4 %fusion.100 = (f32[256,6,7,128]{3,2,1,0:T(8,128)}, f32[256,6,7,128]{3,2,1,0:T(8,128)}) fusion(bf16[256,6,8,128]{3,2,1,0:T(8,128)(2,1)S(1)} %fusion.31), kind=kLoop, calls=%fused_computation.176 | loop fusion | bytes 22020096 | tf_op jit(solution)/shard_map/jit(_roll_static)/slice | solution.py:60
  364.8 5.5 %fusion.101 = (f32[256,6,8,1]{3,2,1,0:T(8,128)}, f32[256,6,8,1]{3,2,1,0:T(8,128)}) fusion(bf16[256,6,8,128]{3,2,1,0:T(8,128)(2,1)S(1)} %fusion.31), kind=kLoop, calls=%fused_computation.177 | loop fusion | bytes 196608 | tf_op jit(solution)/shard_map/jit(_roll_static)/slice | solution.py:65
  370.3 4.7 %slice_convert_fusion.1 = (f32[256,5,8,128]{3,2,1,0:T(8,128)}, f32[256,5,8,128]{3,2,1,0:T(8,128)}) fusion(bf16[256,6,8,128]{3,2,1,0:T(8,128)(2,1)S(1)} %fusion.31), kind=kLoop, calls=%fused_computation.55 | loop fusion | flops 2621440 | bytes 15728640 | tf_op jit(solution)/shard_map/convert_element_type | solution.py:102
  374.9 3.6 fusion.45
  378.6 5.5 %fusion.108 = f32[6144,256]{1,0:T(8,128)} fusion(bf16[6144,256]{1,0:T(8,128)(2,1)} %all-gather.5.cloned.1.call-done, bf16[256,256]{1,0:T(8,128)(2,1)S(1)} %copy-done.3), kind=kOutput, calls=%fused_computation.184 | convolution fusion | flops 805306368 | bytes 9568256 | tf_op jit(solution)/shard_map/dot_general | solution.py:118
  384.0 6.7 %copy.15 = f32[256,6,8,128]{3,2,1,0:T(8,128)} copy(f32[256,6,8,128]{0,3,2,1:T(8,128)} %bitcast.78) | data formatting | bytes 12582912 | tf_op jit(solution)/shard_map/reshape | solution.py:123
  390.7 22.4 %fusion.30 = bf16[256,6,8,128]{3,2,1,0:T(8,128)(2,1)} fusion(f32[256,6,8,128]{3,2,1,0:T(8,128)} %copy.15, f32[256,6,8,1]{3,2,1,0:T(8,128)} %get-tuple-element.18, f32[256,6,8,127]{3,2,1,0:T(8,128)} %get-tuple-element.20, f32[256,6,8,127]{3,2,1,0:T(8,128)} %get-tuple-element.19, f32[256,6,8,1]{3,2,1,0:T(8,128)} %get-tuple-element.17, ...), kind=kLoop, calls=%fused_computation.46 | loop fusion | flops 48758784 | bytes 50338816 | tf_op jit(solution)/shard_map/convert_element_type | solution.py:129
  (48 shorter events, 22.0 us)
Async XLA Ops:
  6.5 0.9 copy-start
  6.5 98.0 %reduce-scatter.3.cloned.1.call-start = ((), (), s32[]{:S(2)}) async-start(), calls=%async_computation.2 | async-start | bytes 6684672 | tf_op jit(solution)/shard_map/reduce_scatter | solution.py:110
  13.3 93.0 %copy-start.2 = (bf16[256,6,8,128]{3,2,1,0:T(8,128)(2,1)S(1)}, bf16[256,6,8,128]{3,2,1,0:T(8,128)(2,1)}, u32[]{:S(2)}) copy-start(bf16[256,6,8,128]{3,2,1,0:T(8,128)(2,1)} %param.5) | copy-start | bytes 9437188
  13.3 166.5 %all-gather.3.cloned.1.call-start = ((), (), s32[]{:S(2)}) async-start(), calls=%async_computation.3 | async-start | bytes 3342336 | tf_op jit(solution)/shard_map/all_gather | solution.py:120
  106.2 199.3 %reduce-scatter.5.cloned.1.call-start = ((), (), s32[]{:S(2)}) async-start(), calls=%async_computation.4 | async-start | bytes 6684672 | tf_op jit(solution)/shard_map/reduce_scatter | solution.py:110
  107.4 67.2 %collective-permute-start = (bf16[256,1,8,128]{3,2,0,1:T(8,128)(2,1)}, bf16[256,1,8,128]{3,2,0,1:T(8,128)(2,1)}, u32[]{:S(2)}, u32[]{:S(2)}) collective-permute-start(bf16[256,1,8,128]{3,2,0,1:T(8,128)(2,1)} %get-tuple-element.21), channel_id=1, source_target_pairs={{0,16},{16,32},{32,48},{48,64},{64,80},{80,96},{96,112},{1,17},{17... | collective-permute-start | bytes 1572872 | tf_op jit(solution)/shard_map/ppermute | solution.py:18
  111.7 65.5 %collective-permute-start.1 = (bf16[256,1,8,128]{3,2,1,0:T(8,128)(2,1)}, bf16[256,1,8,128]{3,2,1,0:T(8,128)(2,1)}, u32[]{:S(2)}, u32[]{:S(2)}) collective-permute-start(bf16[256,1,8,128]{3,2,1,0:T(8,128)(2,1)} %get-tuple-element.22), channel_id=1, source_target_pairs={{16,0},{32,16},{48,32},{64,48},{80,64},{96,80},{112,96},{17,1},{33... | collective-permute-start | bytes 1572872 | tf_op jit(solution)/shard_map/ppermute | solution.py:21
  168.4 6.1 %copy-start.4 = (s32[2,8,128]{2,1,0:T(8,128)S(1)}, s32[2,8,128]{2,1,0:T(8,128)}, u32[]{:S(2)}) copy-start(s32[2,8,128]{2,1,0:T(8,128)} %param.9) | copy-start | bytes 24580
  168.4 11.4 %copy-start.3 = (bf16[256,256]{1,0:T(8,128)(2,1)S(1)}, bf16[256,256]{1,0:T(8,128)(2,1)}, u32[]{:S(2)}) copy-start(bf16[256,256]{1,0:T(8,128)(2,1)} %param.6) | copy-start | bytes 393220
  185.3 6.7 %copy-start.5 = (f32[256]{0:T(256)S(1)}, f32[256]{0:T(256)}, u32[]{:S(2)}) copy-start(f32[256]{0:T(256)} %param.8) | copy-start | bytes 3076
  217.8 160.8 %all-gather.5.cloned.1.call-start = ((), (), s32[]{:S(2)}) async-start(), calls=%async_computation.5 | async-start | bytes 3342336 | tf_op jit(solution)/shard_map/all_gather | solution.py:120
  308.3 66.6 %collective-permute-start.2 = (bf16[256,1,8,128]{3,2,0,1:T(8,128)(2,1)}, bf16[256,1,8,128]{3,2,0,1:T(8,128)(2,1)}, u32[]{:S(2)}, u32[]{:S(2)}) collective-permute-start(bf16[256,1,8,128]{3,2,0,1:T(8,128)(2,1)} %get-tuple-element.9), channel_id=1, source_target_pairs={{0,16},{16,32},{32,48},{48,64},{64,80},{80,96},{96,112},{1,17},{17... | collective-permute-start | bytes 1572872 | tf_op jit(solution)/shard_map/ppermute | solution.py:18
  312.7 62.3 %collective-permute-start.3 = (bf16[256,1,8,128]{3,2,0,1:T(8,128)(2,1)}, bf16[256,1,8,128]{3,2,0,1:T(8,128)(2,1)}, u32[]{:S(2)}, u32[]{:S(2)}) collective-permute-start(bf16[256,1,8,128]{3,2,0,1:T(8,128)(2,1)} %get-tuple-element.10), channel_id=1, source_target_pairs={{16,0},{32,16},{48,32},{64,48},{80,64},{96,80},{112,96},{17,1},{33... | collective-permute-start | bytes 1572872 | tf_op jit(solution)/shard_map/ppermute | solution.py:21
  390.7 22.4 %copy-start.1 = (bf16[256,256]{1,0:T(8,128)(2,1)S(1)}, bf16[256,256]{1,0:T(8,128)(2,1)}, u32[]{:S(2)}) copy-start(bf16[256,256]{1,0:T(8,128)(2,1)} %param.7) | copy-start | bytes 393220
Sparse Core Ops, SparseCore 0:
  13.5 91.0 reduce-scatter.2
  107.0 52.6 all-gather.2
  217.9 87.5 reduce-scatter.4
  307.9 52.6 all-gather.4
where the time goes:
time: 420 us
  waiting for transfers between devices  179 us (43%)
  blocking collectives  70 us (17%)
  other arithmetic  69.8 us (17%)
  local copies, waits for them, and re-layouts  53.4 us (13%)
  matrix products  20.8 us (5%)
  starting transfers between devices  13.4 us (3%)
  between operations  13.3 us (3%)
    reduce_scatter x2, waiting for transfers between devices, body(): lax.psum_scatter(lax.dot_general(flat_rows, down_factor, (((0,), (0,)), (...  179 us
    psum x2, blocking collectives, body(): outflux = lax.psum(jnp.stack([out_low, out_high]), 'vel')  70 us
    convert_element_type x2, other arithmetic, body(): current = updated.astype(jnp.bfloat16)  44.2 us
    slice x4, local copies, waits for them, and re-layouts, transport(): jnp.roll(centre, 1, axis_y)  22 us
    slice x4, local copies, waits for them, and re-layouts, transport(): jnp.roll(centre, 1, axis_x)  15 us
    reshape x2, local copies, waits for them, and re-layouts, body(): gained = lax.dot_general(up_factor, lax.all_gather(coeffs, 'vel', axis=0,...  13.4 us
    dot_general x2, matrix products, body(): lax.dot_general(up_factor, lax.all_gather(coeffs, 'vel', axis=0, tiled=Tr...  11 us
    dot_general x2, matrix products, body(): lax.dot_general(flat_rows, down_factor, (((0,), (0,)), ((), ())), preferr...  9.85 us
  transfers between devices with their start and end apart: 8, of which 2 were waited for; matrix products, arithmetic and copies ran while one was open for 15% of the time, Pallas kernels for 0%

commit v1 on v0

--- a/solution.py
+++ b/solution.py
@@ -90,7 +90,7 @@
         high_face = current[:, depth - 1].astype(jnp.float32)
         out_low = jnp.sum(jnp.maximum(-along_z, 0.0)[:, None, None] * low_face, axis=0)
         out_high = jnp.sum(jnp.maximum(along_z, 0.0)[:, None, None] * high_face, axis=0)
-        outflux = lax.psum(jnp.stack([out_low, out_high]), "vel")
+        outflux = jnp.sum(lax.all_gather(jnp.stack([out_low, out_high]), "vel"), axis=0)
         ghost_low = wall_ghost(outflux[0], wall_kind[0], maxwell, energy, norm)
         ghost_high = wall_ghost(outflux[1], wall_kind[1], maxwell, energy, norm)
         padded = with_halo(current, (("space", 1),), 1)

time: 420 us -> 401 us (0.955)
  blocking collectives: 70 us -> 45.6 us
  waiting for transfers between devices: 179 us -> 186 us
    psum x2 -> x0, blocking collectives: 70 us -> none  [body(): outflux = lax.psum(jnp.stack([out_low, out_high]), 'vel')]
    all_gather x0 -> x2, blocking collectives: none -> 45.6 us  [body(): lax.all_gather(jnp.stack([out_low, out_high]), 'vel')]
    ppermute x2, waiting for transfers between devices: 0.01 us -> 7.03 us  [with_halo(): lax.ppermute(lax.slice_in_dim(block, 0, width, axis=dim), axis, backward)]
  transfers between devices with their start and end apart: 8 -> 8, of which waited for: 2 -> 3; matrix products, arithmetic and copies ran while one was open for 15% -> 15% of each run, Pallas kernels for 0% -> 0%
where the time goes in v1:
time: 401 us; the launch traced here: 400 us
  waiting for transfers between devices  186 us (46%)
  other arithmetic  68.8 us (17%)
  local copies, waits for them, and re-layouts  52.5 us (13%)
  blocking collectives  45.6 us (11%)
  matrix products  20.8 us (5%)
  between operations  13.3 us (3%)
  starting transfers between devices  12.6 us (3%)
    reduce_scatter x2, waiting for transfers between devices, body(): lax.psum_scatter(lax.dot_general(flat_rows, down_factor, (((0,), (0,)), (...  179 us
    all_gather x2, blocking collectives, body(): lax.all_gather(jnp.stack([out_low, out_high]), 'vel')  45.6 us
    convert_element_type x2, other arithmetic, body(): current = updated.astype(jnp.bfloat16)  44.4 us
    slice x4, local copies, waits for them, and re-layouts, transport(): jnp.roll(centre, 1, axis_y)  22 us
    slice x4, local copies, waits for them, and re-layouts, transport(): jnp.roll(centre, 1, axis_x)  15.1 us
    reshape x2, local copies, waits for them, and re-layouts, body(): gained = lax.dot_general(up_factor, lax.all_gather(coeffs, 'vel', axis=0,...  13.4 us
    dot_general x2, matrix products, body(): lax.dot_general(up_factor, lax.all_gather(coeffs, 'vel', axis=0, tiled=Tr...  11 us
    dot_general x2, matrix products, body(): lax.dot_general(flat_rows, down_factor, (((0,), (0,)), ((), ())), preferr...  9.85 us
  transfers between devices with their start and end apart: 8, of which 3 were waited for; matrix products, arithmetic and copies ran while one was open for 15% of the time, Pallas kernels for 0%

profile of v1, /device:TPU:8, one launch (start us, length us, event | category | flops | bytes accessed | tf_op | source)
XLA Modules:
  0.0 399.9 jit_solution(12482998584844061255)
XLA Ops:
  7.4 5.9 %fusion.35 = f32[6144,256]{1,0:T(8,128)} fusion(bf16[256,256]{1,0:T(8,128)(2,1)S(1)} %copy-done, bf16[32,8,48,128]{3,2,1,0:T(8,128)(2,1)} %bitcast.78), kind=kOutput, calls=%fused_computation.51 | convolution fusion | flops 805306368 | bytes 9568256 | tf_op jit(solution)/shard_map/dot_general | solution.py:111
  13.4 91.1 %reduce-scatter.3.cloned.1.call-done = f32[384,256]{1,0:T(8,128)} async-done(((f32[6144,256]{1,0:T(8,128)}), f32[384,256]{1,0:T(8,128)}) %reduce-scatter.3.cloned.1.call-update) | async-done | bytes 393232 | tf_op jit(solution)/shard_map/reduce_scatter | solution.py:110
  107.4 4.3 %collective-permute-start = (bf16[256,1,8,128]{3,2,0,1:T(8,128)(2,1)}, bf16[256,1,8,128]{3,2,0,1:T(8,128)(2,1)}, u32[]{:S(2)}, u32[]{:S(2)}) collective-permute-start(bf16[256,1,8,128]{3,2,0,1:T(8,128)(2,1)} %get-tuple-element.21), channel_id=1, source_target_pairs={{0,16},{16,32},{32,48},{48,64},{64,80},{80,96},{96,112},{1,17},{17... | collective-permute-start | bytes 1572872 | tf_op jit(solution)/shard_map/ppermute | solution.py:18
  115.0 23.0 %all-gather = f32[32,8,128]{2,1,0:T(8,128)S(1)} all-gather(f32[2,8,128]{2,1,0:T(8,128)S(1)} %pad_maximum_fusion), channel_id=2, replica_groups=mesh['space'=8,'vel'=16] {'vel'}, dimensions={0}, use_global_device_ids=true | all-gather | bytes 139264 | tf_op jit(solution)/shard_map/all_gather | solution.py:93
  138.8 4.7 %slice_convert_fusion.3 = (f32[256,5,8,128]{3,2,1,0:T(8,128)}, f32[256,5,8,128]{3,2,1,0:T(8,128)}) fusion(bf16[256,6,8,128]{3,2,1,0:T(8,128)(2,1)S(1)} %copy-done.2), kind=kLoop, calls=%fused_computation.57 | loop fusion | flops 2621440 | bytes 15728640 | tf_op jit(solution)/shard_map/convert_element_type | solution.py:102
  145.5 5.5 %fusion.106 = (f32[256,6,8,127]{3,2,1,0:T(8,128)}, f32[256,6,8,127]{3,2,1,0:T(8,128)}) fusion(bf16[256,6,8,128]{3,2,1,0:T(8,128)(2,1)S(1)} %copy-done.2), kind=kLoop, calls=%fused_computation.182 | loop fusion | bytes 24969216 | tf_op jit(solution)/shard_map/jit(_roll_static)/slice | solution.py:65
  151.0 5.6 %fusion.105 = (f32[256,6,8,1]{3,2,1,0:T(8,128)}, f32[256,6,8,1]{3,2,1,0:T(8,128)}) fusion(bf16[256,6,8,128]{3,2,1,0:T(8,128)(2,1)S(1)} %copy-done.2), kind=kLoop, calls=%fused_computation.181 | loop fusion | bytes 196608 | tf_op jit(solution)/shard_map/jit(_roll_static)/slice | solution.py:65
  156.6 5.4 %fusion.104 = (f32[256,6,7,128]{3,2,1,0:T(8,128)}, f32[256,6,7,128]{3,2,1,0:T(8,128)}) fusion(bf16[256,6,8,128]{3,2,1,0:T(8,128)(2,1)S(1)} %copy-done.2), kind=kLoop, calls=%fused_computation.180 | loop fusion | bytes 22020096 | tf_op jit(solution)/shard_map/jit(_roll_static)/slice | solution.py:60
  165.4 2.6 fusion.49
  168.0 5.5 %fusion.107 = f32[6144,256]{1,0:T(8,128)} fusion(bf16[6144,256]{1,0:T(8,128)(2,1)} %all-gather.5.cloned.1.call-done, bf16[256,256]{1,0:T(8,128)(2,1)S(1)} %copy-done.3), kind=kOutput, calls=%fused_computation.183 | convolution fusion | flops 805306368 | bytes 9568256 | tf_op jit(solution)/shard_map/dot_general | solution.py:118
  173.5 6.7 %copy.20 = f32[256,6,8,128]{3,2,1,0:T(8,128)} copy(f32[256,6,8,128]{0,3,2,1:T(8,128)} %bitcast.79) | data formatting | bytes 12582912 | tf_op jit(solution)/shard_map/reshape | solution.py:123
  180.2 22.0 %fusion.31 = bf16[256,6,8,128]{3,2,1,0:T(8,128)(2,1)S(1)} fusion(f32[256,6,8,128]{3,2,1,0:T(8,128)} %copy.20, f32[256,6,8,1]{3,2,1,0:T(8,128)} %get-tuple-element.30, f32[256,6,8,127]{3,2,1,0:T(8,128)} %get-tuple-element.32, f32[256,6,8,127]{3,2,1,0:T(8,128)} %get-tuple-element.31, f32[256,6,8,1]{3,2,1,0:T(8,128)} %get-tuple-element.29, ...), kind=kLoop, calls=%fused_computation.47 | loop fusion | flops 48758784 | bytes 50338816 | tf_op jit(solution)/shard_map/convert_element_type | solution.py:129
  202.2 4.0 fusion.32
  206.2 88.0 %reduce-scatter.5.cloned.1.call-done = f32[384,256]{1,0:T(8,128)} async-done(((f32[6144,256]{1,0:T(8,128)}), f32[384,256]{1,0:T(8,128)}) %reduce-scatter.5.cloned.1.call-update) | async-done | bytes 393232 | tf_op jit(solution)/shard_map/reduce_scatter | solution.py:110
  297.0 22.6 %all-gather.1 = f32[32,8,128]{2,1,0:T(8,128)S(1)} all-gather(f32[2,8,128]{2,1,0:T(8,128)S(1)} %pad_maximum_fusion.1), channel_id=3, replica_groups=mesh['space'=8,'vel'=16] {'vel'}, dimensions={0}, use_global_device_ids=true | all-gather | bytes 139264 | tf_op jit(solution)/shard_map/all_gather | solution.py:93
  319.6 3.4 collective-permute-start.2
  328.3 5.5 %fusion.102 = (f32[256,6,8,127]{3,2,1,0:T(8,128)}, f32[256,6,8,127]{3,2,1,0:T(8,128)}) fusion(bf16[256,6,8,128]{3,2,1,0:T(8,128)(2,1)S(1)} %fusion.31), kind=kLoop, calls=%fused_computation.178 | loop fusion | bytes 24969216 | tf_op jit(solution)/shard_map/jit(_roll_static)/slice | solution.py:65
  333.7 5.4 %fusion.100 = (f32[256,6,7,128]{3,2,1,0:T(8,128)}, f32[256,6,7,128]{3,2,1,0:T(8,128)}) fusion(bf16[256,6,8,128]{3,2,1,0:T(8,128)(2,1)S(1)} %fusion.31), kind=kLoop, calls=%fused_computation.176 | loop fusion | bytes 22020096 | tf_op jit(solution)/shard_map/jit(_roll_static)/slice | solution.py:60
  339.2 5.5 %fusion.101 = (f32[256,6,8,1]{3,2,1,0:T(8,128)}, f32[256,6,8,1]{3,2,1,0:T(8,128)}) fusion(bf16[256,6,8,128]{3,2,1,0:T(8,128)(2,1)S(1)} %fusion.31), kind=kLoop, calls=%fused_computation.177 | loop fusion | bytes 196608 | tf_op jit(solution)/shard_map/jit(_roll_static)/slice | solution.py:65
  344.7 4.7 %slice_convert_fusion.1 = (f32[256,5,8,128]{3,2,1,0:T(8,128)}, f32[256,5,8,128]{3,2,1,0:T(8,128)}) fusion(bf16[256,6,8,128]{3,2,1,0:T(8,128)(2,1)S(1)} %fusion.31), kind=kLoop, calls=%fused_computation.55 | loop fusion | flops 2621440 | bytes 15728640 | tf_op jit(solution)/shard_map/convert_element_type | solution.py:102
  349.4 7.0 %collective-permute-done.3 = bf16[256,1,8,128]{3,2,0,1:T(8,128)(2,1)S(1)} collective-permute-done((bf16[256,1,8,128]{3,2,0,1:T(8,128)(2,1)S(1)}, bf16[256,1,8,128]{3,2,0,1:T(8,128)(2,1)S(1)}, u32[]{:S(2)}, u32[]{:S(2)}) %collective-permute-start.3) | collective-permute-done | bytes 524320 | tf_op jit(solution)/shard_map/ppermute | solution.py:21
  358.8 5.5 %fusion.108 = f32[6144,256]{1,0:T(8,128)} fusion(bf16[6144,256]{1,0:T(8,128)(2,1)} %all-gather.7.cloned.1.call-done, bf16[256,256]{1,0:T(8,128)(2,1)S(1)} %copy-done.3), kind=kOutput, calls=%fused_computation.184 | convolution fusion | flops 805306368 | bytes 9568256 | tf_op jit(solution)/shard_map/dot_general | solution.py:118
  364.3 6.7 %copy.25 = f32[256,6,8,128]{3,2,1,0:T(8,128)} copy(f32[256,6,8,128]{0,3,2,1:T(8,128)} %bitcast.80) | data formatting | bytes 12582912 | tf_op jit(solution)/shard_map/reshape | solution.py:123
  370.9 22.4 %fusion.30 = bf16[256,6,8,128]{3,2,1,0:T(8,128)(2,1)} fusion(f32[256,6,8,128]{3,2,1,0:T(8,128)} %copy.25, f32[256,6,8,1]{3,2,1,0:T(8,128)} %get-tuple-element.18, f32[256,6,8,127]{3,2,1,0:T(8,128)} %get-tuple-element.20, f32[256,6,8,127]{3,2,1,0:T(8,128)} %get-tuple-element.19, f32[256,6,8,1]{3,2,1,0:T(8,128)} %get-tuple-element.17, ...), kind=kLoop, calls=%fused_computation.46 | loop fusion | flops 48758784 | bytes 50338816 | tf_op jit(solution)/shard_map/convert_element_type | solution.py:129
  (50 shorter events, 23.6 us)
Async XLA Ops:
  6.5 0.9 copy-start
  6.5 98.0 %reduce-scatter.3.cloned.1.call-start = ((), (), s32[]{:S(2)}) async-start(), calls=%async_computation.2 | async-start | bytes 6684672 | tf_op jit(solution)/shard_map/reduce_scatter | solution.py:110
  13.3 93.0 %copy-start.2 = (bf16[256,6,8,128]{3,2,1,0:T(8,128)(2,1)S(1)}, bf16[256,6,8,128]{3,2,1,0:T(8,128)(2,1)}, u32[]{:S(2)}) copy-start(bf16[256,6,8,128]{3,2,1,0:T(8,128)(2,1)} %param.5) | copy-start | bytes 9437188
  13.3 154.6 %all-gather.5.cloned.1.call-start = ((), (), s32[]{:S(2)}) async-start(), calls=%async_computation.3 | async-start | bytes 3342336 | tf_op jit(solution)/shard_map/all_gather | solution.py:120
  106.2 188.0 %reduce-scatter.5.cloned.1.call-start = ((), (), s32[]{:S(2)}) async-start(), calls=%async_computation.4 | async-start | bytes 6684672 | tf_op jit(solution)/shard_map/reduce_scatter | solution.py:110
  107.4 55.4 %collective-permute-start = (bf16[256,1,8,128]{3,2,0,1:T(8,128)(2,1)}, bf16[256,1,8,128]{3,2,0,1:T(8,128)(2,1)}, u32[]{:S(2)}, u32[]{:S(2)}) collective-permute-start(bf16[256,1,8,128]{3,2,0,1:T(8,128)(2,1)} %get-tuple-element.21), channel_id=1, source_target_pairs={{0,16},{16,32},{32,48},{48,64},{64,80},{80,96},{96,112},{1,17},{17... | collective-permute-start | bytes 1572872 | tf_op jit(solution)/shard_map/ppermute | solution.py:18
  111.7 53.7 %collective-permute-start.1 = (bf16[256,1,8,128]{3,2,1,0:T(8,128)(2,1)}, bf16[256,1,8,128]{3,2,1,0:T(8,128)(2,1)}, u32[]{:S(2)}, u32[]{:S(2)}) collective-permute-start(bf16[256,1,8,128]{3,2,1,0:T(8,128)(2,1)} %get-tuple-element.22), channel_id=1, source_target_pairs={{16,0},{32,16},{48,32},{64,48},{80,64},{96,80},{112,96},{17,1},{33... | collective-permute-start | bytes 1572872 | tf_op jit(solution)/shard_map/ppermute | solution.py:21
  156.6 6.1 %copy-start.4 = (s32[2,8,128]{2,1,0:T(8,128)S(1)}, s32[2,8,128]{2,1,0:T(8,128)}, u32[]{:S(2)}) copy-start(s32[2,8,128]{2,1,0:T(8,128)} %param.9) | copy-start | bytes 24580
  156.6 11.4 %copy-start.3 = (bf16[256,256]{1,0:T(8,128)(2,1)S(1)}, bf16[256,256]{1,0:T(8,128)(2,1)}, u32[]{:S(2)}) copy-start(bf16[256,256]{1,0:T(8,128)(2,1)} %param.6) | copy-start | bytes 393220
  173.5 6.7 %copy-start.5 = (f32[256]{0:T(256)S(1)}, f32[256]{0:T(256)}, u32[]{:S(2)}) copy-start(f32[256]{0:T(256)} %param.8) | copy-start | bytes 3076
  206.2 152.6 %all-gather.7.cloned.1.call-start = ((), (), s32[]{:S(2)}) async-start(), calls=%async_computation.5 | async-start | bytes 3342336 | tf_op jit(solution)/shard_map/all_gather | solution.py:120
  319.6 29.7 %collective-permute-start.2 = (bf16[256,1,8,128]{3,2,0,1:T(8,128)(2,1)S(1)}, bf16[256,1,8,128]{3,2,0,1:T(8,128)(2,1)S(1)}, u32[]{:S(2)}, u32[]{:S(2)}) collective-permute-start(bf16[256,1,8,128]{3,2,0,1:T(8,128)(2,1)S(1)} %get-tuple-element.9), channel_id=1, source_target_pairs={{0,16},{16,32},{32,48},{48,64},{64,80},{80,96},{96,112},{1,17},{17... | collective-permute-start | bytes 1572872 | tf_op jit(solution)/shard_map/ppermute | solution.py:18
  323.0 33.4 %collective-permute-start.3 = (bf16[256,1,8,128]{3,2,0,1:T(8,128)(2,1)S(1)}, bf16[256,1,8,128]{3,2,0,1:T(8,128)(2,1)S(1)}, u32[]{:S(2)}, u32[]{:S(2)}) collective-permute-start(bf16[256,1,8,128]{3,2,0,1:T(8,128)(2,1)S(1)} %get-tuple-element.10), channel_id=1, source_target_pairs={{16,0},{32,16},{48,32},{64,48},{80,64},{96,80},{112,96},{17,1},{33... | collective-permute-start | bytes 1572872 | tf_op jit(solution)/shard_map/ppermute | solution.py:21
  370.9 22.4 %copy-start.1 = (bf16[256,256]{1,0:T(8,128)(2,1)S(1)}, bf16[256,256]{1,0:T(8,128)(2,1)}, u32[]{:S(2)}) copy-start(bf16[256,256]{1,0:T(8,128)(2,1)} %param.7) | copy-start | bytes 393220
Sparse Core Ops, SparseCore 0:
  13.5 91.0 reduce-scatter.2
  107.0 52.7 all-gather.4
  206.3 87.8 reduce-scatter.4
  296.5 59.5 all-gather.6
